TPU v7x, 128 devices: a whole 4x4x4 slice. The times are simulated.
128 devices in a mesh: row: 8 (over z, core), col: 8 (over x, y_lo), depth: 2 (over y_hi).
Axes of the slice: x: 4, y: 4 (y_hi: 2, y_lo: 2; y = y_hi * 2 + y_lo), z: 4, core: 2. Of those that a mesh axis runs over, the one named last changes fastest.
Arguments:
- hidden_state: bfloat16 [2048, 8192], P(('col', 'depth'), 'row'), may hold values from -110 to 110
- norm_gain: float32 [8192], P('row'), may hold values from 0.1 to 1.9
- gate_up_weight: bfloat16 [8192, 2, 28672], P('row', None, ('col', 'depth')), may hold values from -0.0625 to 0.0625
- down_weight: bfloat16 [28672, 8192], P(('col', 'depth'), 'row'), may hold values from -0.03125 to 0.03125
Outputs:
- block_output: bfloat16 [2048, 8192], P(('col', 'depth'), 'row')
All inputs are finite; a program needn't handle non-finite values.
Results may differ from a plain program's by a relative error of at most 0.014.
Values may be sent and summed in bfloat16 or wider, within the bound.
A program may use at most 128 MiB of HBM per device.

v0:
```python
import jax
import jax.numpy as jnp
from jax import lax
from jax.sharding import PartitionSpec as P

D = 8192


def local(hidden_state, norm_gain, gate_up_weight, down_weight):
    wide = hidden_state.astype(jnp.float32)
    squares = lax.psum(jnp.sum(wide * wide, axis=1), "row")
    scale = lax.rsqrt(squares / D + 1e-05)
    normed = (wide * scale[:, None] * norm_gain[None, :]).astype(jnp.bfloat16)
    partial_sums = jnp.einsum(
        "td,dkf->tkf",
        lax.all_gather(normed, ("col", "depth"), axis=0, tiled=True),
        gate_up_weight,
        preferred_element_type=jnp.float32,
    )
    shares = lax.psum_scatter(
        partial_sums.astype(jnp.bfloat16), "row", scatter_dimension=0, tiled=True
    ).astype(jnp.float32)
    hidden = (jax.nn.silu(shares[:, 0]) * shares[:, 1]).astype(jnp.bfloat16)
    terms = jnp.dot(
        lax.all_gather(hidden, "row", axis=0, tiled=True),
        down_weight,
        preferred_element_type=jnp.float32,
    )
    branch = lax.psum_scatter(
        terms.astype(jnp.bfloat16), ("col", "depth"), scatter_dimension=0, tiled=True
    ).astype(jnp.float32)
    return (wide + branch).astype(jnp.bfloat16)


def solution(mesh):
    return jax.shard_map(
        local,
        mesh=mesh,
        in_specs=(
            P(("col", "depth"), "row"),
            P("row"),
            P("row", None, ("col", "depth")),
            P(("col", "depth"), "row"),
        ),
        out_specs=P(("col", "depth"), "row"),
        check_vma=False,
    )
```

profile of v0, /device:TPU:0, one launch (start us, length us, event | category | flops | bytes accessed | tf_op | source)
XLA Modules:
  0.0 396.0 jit_solution(1344691857680732506)
XLA Ops:
  6.5 0.0 all-gather.3.cloned.1.call-start
  6.5 1.1 fusion.4
  7.6 16.0 %psum.7 = f32[128]{0:T(128)S(1)} all-reduce(f32[128]{0:T(128)S(1)} %fusion.4), channel_id=1, replica_groups=mesh['row'=8,'col'=8,'depth'=2] {'row'}, use_global_device_ids=true, to_apply=%region_1.0 | all-reduce | flops 128 | bytes 1024 | tf_op jit(solution)/shard_map/psum | solution.py:11
  23.6 1.8 fusion.6
  25.4 0.0 all-gather.3.cloned.1.call-update
  25.4 0.0 reduce-scatter.3.cloned.1.call-start
  25.5 97.5 %all-gather.3.cloned.1.call-done = bf16[2048,1024]{1,0:T(8,128)(2,1)} async-done(((bf16[128,1024]{1,0:T(8,128)(2,1)}), bf16[2048,1024]{1,0:T(8,128)(2,1)}) %all-gather.3.cloned.1.call-update) | async-done | bytes 4194320 | tf_op jit(solution)/shard_map/all_gather | solution.py:16
  123.0 22.3 %convolution_convert_fusion = bf16[2048,2,1792]{2,0,1:T(8,128)(2,1)} fusion(bf16[1024,2,1792]{2,1,0:T(2,128)(2,1)} %param.6, bf16[2048,1024]{1,0:T(8,128)(2,1)} %all-gather.3.cloned.1.call-done), kind=kOutput, calls=%fused_computation | convolution fusion | flops 15039725568 | bytes 26214400 | tf_op jit(solution)/shard_map/td,dkf->tkf/dot_general | solution.py:14
  145.2 0.0 reduce-scatter.3.cloned.1.call-update
  145.3 0.0 all-gather.5.cloned.1.call-start
  145.3 81.3 %reduce-scatter.3.cloned.1.call-done = bf16[256,2,1792]{2,0,1:T(8,128)(2,1)} async-done(((bf16[2048,2,1792]{2,0,1:T(8,128)(2,1)}), bf16[256,2,1792]{2,0,1:T(8,128)(2,1)}) %reduce-scatter.3.cloned.1.call-update) | async-done | bytes 1835024 | tf_op jit(solution)/shard_map/reduce_scatter | solution.py:20
  226.6 1.8 convert_element_type.27
  228.4 1.5 fusion.3
  229.9 0.0 all-gather.5.cloned.1.call-update
  229.9 0.0 reduce-scatter.5.cloned.1.call-start
  229.9 45.1 %all-gather.5.cloned.1.call-done = bf16[2048,1792]{1,0:T(8,128)(2,1)} async-done(((bf16[256,1792]{1,0:T(8,128)(2,1)}), bf16[2048,1792]{1,0:T(8,128)(2,1)}) %all-gather.5.cloned.1.call-update) | async-done | bytes 7340048 | tf_op jit(solution)/shard_map/all_gather | solution.py:25
  275.0 12.4 %convolution_convert_fusion.1 = bf16[2048,1024]{1,0:T(8,128)(2,1)} fusion(bf16[2048,1792]{1,0:T(8,128)(2,1)} %all-gather.5.cloned.1.call-done, bf16[1792,1024]{1,0:T(8,128)(2,1)} %param.7), kind=kOutput, calls=%fused_computation.3 | convolution fusion | flops 7518289920 | bytes 15204352 | tf_op jit(solution)/shard_map/dot_general | solution.py:24
  287.4 0.0 copy-start
  287.4 0.0 reduce-scatter.5.cloned.1.call-update
  287.5 100.3 %reduce-scatter.5.cloned.1.call-done = bf16[128,1024]{1,0:T(8,128)(2,1)} async-done(((bf16[2048,1024]{1,0:T(8,128)(2,1)}), bf16[128,1024]{1,0:T(8,128)(2,1)}) %reduce-scatter.5.cloned.1.call-update) | async-done | bytes 262160 | tf_op jit(solution)/shard_map/reduce_scatter | solution.py:29
  387.7 0.0 copy-done
  387.7 1.7 fusion.7
  (1 shorter events, 0.0 us)
Async XLA Ops:
  6.5 116.5 %all-gather.3.cloned.1.call-start = ((), (), s32[]{:S(2)}) async-start(), calls=%async_computation.2 | async-start | bytes 4456448 | tf_op jit(solution)/shard_map/all_gather | solution.py:16
  25.4 201.2 %reduce-scatter.3.cloned.1.call-start = ((), (), s32[]{:S(2)}) async-start(), calls=%async_computation.3 | async-start | bytes 16515072 | tf_op jit(solution)/shard_map/reduce_scatter | solution.py:20
  145.3 129.8 %all-gather.5.cloned.1.call-start = ((), (), s32[]{:S(2)}) async-start(), calls=%async_computation.4 | async-start | bytes 8257536 | tf_op jit(solution)/shard_map/all_gather | solution.py:25
  229.9 157.8 %reduce-scatter.5.cloned.1.call-start = ((), (), s32[]{:S(2)}) async-start(), calls=%async_computation.5 | async-start | bytes 4456448 | tf_op jit(solution)/shard_map/reduce_scatter | solution.py:29
  287.4 100.3 %copy-start = (bf16[128,1024]{1,0:T(8,128)(2,1)S(1)}, bf16[128,1024]{1,0:T(8,128)(2,1)}, u32[]{:S(2)}) copy-start(bf16[128,1024]{1,0:T(8,128)(2,1)} %param.4) | copy-start | bytes 786436
Sparse Core Ops, SparseCore 0:
  25.5 97.4 all-gather.2
  145.4 81.1 reduce-scatter.2
  230.0 44.9 all-gather.4
  287.6 100.1 reduce-scatter.4
where the time goes:
time: 396 us
  waiting for transfers between devices  324 us (82%)
  matrix products  34.6 us (9%)
  blocking collectives  16 us (4%)
  between operations  13.1 us (3%)
  other arithmetic  7.84 us (2%)
    reduce_scatter x1, waiting for transfers between devices, local(): lax.psum_scatter(terms.astype(jnp.bfloat16), ('col', 'depth'), scatter_di...  100 us
    all_gather x1, waiting for transfers between devices, local(): lax.all_gather(normed, ('col', 'depth'), axis=0, tiled=True)  97.5 us
    reduce_scatter x1, waiting for transfers between devices, local(): lax.psum_scatter(partial_sums.astype(jnp.bfloat16), 'row', scatter_dimens...  81.3 us
    all_gather x1, waiting for transfers between devices, local(): lax.all_gather(hidden, 'row', axis=0, tiled=True)  45.1 us
    dot_general x1, matrix products, local(): jnp.einsum('td,dkf->tkf', lax.all_gather(normed, ('col', 'depth'), axis=0...  22.3 us
    psum x1, blocking collectives, local(): squares = lax.psum(jnp.sum(wide * wide, axis=1), 'row')  16 us
    dot_general x1, matrix products, local(): jnp.dot(lax.all_gather(hidden, 'row', axis=0, tiled=True), down_weight, p...  12.4 us
  transfers between devices with their start and end apart: 4, of which 4 were waited for; matrix products, arithmetic and copies ran while one was open for 0% of the time, Pallas kernels for 0%

commit v1 on v0

v1 whole, which is shorter than its diff:
```python
import functools

import jax
import jax.numpy as jnp
from jax import lax
from jax.experimental import pallas as pl
from jax.experimental.pallas import tpu as pltpu
from jax.sharding import PartitionSpec as P

D = 8192
TOK = 128
KB = 1024
FH = 896
STEPS = 16
ROWS = TOK // 4
LAST = STEPS - 1
MESH = pl.DeviceIdType.MESH
BF, F32 = jnp.bfloat16, jnp.float32


def kernel(
    h_ref, gain_ref, wt_ref, wd_ref, out_ref,
    a, w, wd, s, br, cs, hid, ds, dr, acc, sq,
    sq_send, sq_recv, a_send, a_recv, as_send, as_recv,
    w_local, w_send, w_recv, wd_sem,
    b_send, b_recv, c_send, c_recv, cs_send, hs_send, hs_recv, d_send, d_recv,
):
    col, depth, row = lax.axis_index("col"), lax.axis_index("depth"), lax.axis_index("row")
    x, y = col // 2, depth * 2 + col % 2
    z, c = row // 2, row % 2

    def at_xy(nx, ny):
        nx, ny = lax.rem(nx + 8, 4), lax.rem(ny + 8, 4)
        return {"col": nx * 2 + ny % 2, "depth": ny // 2}

    def at_z(d, other=0):
        core = c if not other else 1 - c
        return {"row": lax.rem(z + d + 4, 4) * 2 + core}

    sibling = at_z(0, 1)

    def prim(d):
        return at_xy(x + d * (1 - c), y + d * c)

    def sec(d):
        return at_xy(x + d * c, y + d * (1 - c))

    def slot(p, q):
        dx = p * (1 - c) + q * c
        dy = q * (1 - c) + p * c
        return lax.rem(dx + 4 * dy + 15, 16)

    def rdma(src, dst, ssem, rsem, dev):
        return pltpu.make_async_remote_copy(
            src_ref=src, dst_ref=dst, send_sem=ssem, recv_sem=rsem, device_id=dev, device_id_type=MESH
        )

    def wait_recv(ref, sem, dev=sibling):
        rdma(ref, ref, a_send, sem, dev).wait_recv()

    def wait_send(ref, sem, dev=sibling):
        rdma(ref, ref, sem, sem, dev).wait_send()

    barrier = pltpu.get_barrier_semaphore()
    peers = [at_xy(x + o % 4, y + o // 4) for o in range(1, 16)]
    rows = [{"row": lax.rem(row + d, 8)} for d in range(1, 8)]

    own_w = [
        pltpu.make_async_copy(
            wt_ref.at[g, :, pl.ds(pl.multiple_of(c * FH, 128), FH)],
            w.at[c, :, g * FH:(g + 1) * FH],
            w_local.at[g],
        )
        for g in range(2)
    ]
    for copy in own_w:
        copy.start()
    own_wd = pltpu.make_async_copy(wd_ref, wd, wd_sem)
    own_wd.start()

    for dev in peers + rows:
        pl.semaphore_signal(barrier, inc=1, device_id=dev, device_id_type=MESH)

    part = jnp.zeros((TOK, 128), F32)
    for k in range(KB // 128):
        v = h_ref[:, k * 128:(k + 1) * 128].astype(F32)
        acc[:, k * 128:(k + 1) * 128] = v
        part = part + v * v
    sums = jnp.sum(part.T, axis=0, keepdims=True)
    sq[row] = jnp.broadcast_to(sums, (8, 128))

    pl.semaphore_wait(barrier, len(peers) + len(rows))

    for dev in rows:
        rdma(sq.at[row], sq.at[row], sq_send, sq_recv.at[row], dev).start()
    for g in range(2):
        rdma(
            wt_ref.at[g, :, pl.ds(pl.multiple_of((1 - c) * FH, 128), FH)],
            w.at[c, :, g * FH:(g + 1) * FH],
            w_send.at[g],
            w_recv.at[g],
            sibling,
        ).start()
    for d in range(1, 8):
        r = lax.rem(row + d, 8)
        wait_recv(sq.at[r], sq_recv.at[r])
    total = sq[0]
    for r in range(1, 8):
        total = total + sq[r]
    scale = lax.rsqrt(total[0:1] / D + 1e-05)
    scale = jnp.broadcast_to(scale, (128, 128)).T
    for k in range(KB // 128):
        cols = slice(k * 128, (k + 1) * 128)
        a[LAST, c, :, cols] = (acc[:, cols] * scale * gain_ref[0:1, cols]).astype(BF)

    half = TOK // 2

    def whole(src, dst, dev):
        rdma(a.at[src, c], a.at[dst, c], a_send, a_recv.at[dst, 0], dev).start()

    def piece(src, dst, dev, n):
        r = slice(n * half, (n + 1) * half)
        rdma(a.at[src, c, r], a.at[dst, c, r], a_send, a_recv.at[dst, n], dev).start()

    def share(src):
        rdma(a.at[src, c], a.at[src, c], as_send, as_recv.at[src], sibling).start()

    def got(at):
        wait_recv(a.at[at, c], a_recv.at[at, 0])

    def got_halves(at):
        for n in range(2):
            wait_recv(a.at[at, c, n * half:(n + 1) * half], a_recv.at[at, n])

    def spread(p):
        at = slot(p, 0)
        whole(at, slot(p, 3), sec(1))
        whole(at, slot(p, 1), sec(-1))

    def turn(p, q):
        at = slot(p, q)
        got(at)
        share(at)
        if q == 1:
            piece(at, slot(p, 2), sec(-1), 0)
        else:
            piece(at, slot(p, 2), sec(1), 1)

    whole(LAST, slot(3, 0), prim(1))
    whole(LAST, slot(1, 0), prim(-1))
    spread(0)
    share(LAST)

    def events0():
        for p in (1, 3):
            at = slot(p, 0)
            got(at)
            share(at)
            if p == 1:
                piece(at, slot(2, 0), prim(-1), 0)
            else:
                piece(at, slot(2, 0), prim(1), 1)
        for q in (1, 3):
            turn(0, q)
        for p in (1, 3):
            spread(p)

    def events1():
        got_halves(slot(2, 0))
        share(slot(2, 0))
        spread(2)
        got_halves(slot(0, 2))
        share(slot(0, 2))

    def events2():
        for p in (1, 3):
            for q in (1, 3):
                turn(p, q)

    def events3():
        for q in (1, 3):
            turn(2, q)
        for p in (1, 3):
            got_halves(slot(p, 2))
            share(slot(p, 2))

    def events4():
        got_halves(slot(2, 2))
        share(slot(2, 2))

    events0()
    for copy in own_w:
        copy.wait()
    for g in range(2):
        wait_recv(w.at[1 - c, :, g * FH:(g + 1) * FH], w_recv.at[g])

    def rows_of(d):
        return pl.ds(pl.multiple_of(lax.rem(z + d + 4, 4) * ROWS, ROWS), ROWS)

    gate, up = slice(0, FH), slice(FH, 2 * FH)
    mine = pl.ds(pl.multiple_of(c * FH, 128), FH)

    def first_matmul(i):
        wait_recv(a.at[i, 1 - c], as_recv.at[i])

        @pl.loop(0, 2 * FH // 256)
        def _(n):
            cols = pl.ds(pl.multiple_of(n * 256, 256), 256)
            p = jnp.dot(a[i, 0], w[0, :, cols], preferred_element_type=F32)
            p += jnp.dot(a[i, 1], w[1, :, cols], preferred_element_type=F32)
            s[i, :, cols] = p.astype(BF)

        rdma(s.at[i, rows_of(2), gate], br.at[i, 0], b_send, b_recv.at[i, 0], at_z(1)).start()
        rdma(s.at[i, rows_of(2), up], br.at[i, 1], b_send, b_recv.at[i, 1], at_z(-1)).start()
        rdma(s.at[i, rows_of(1), up], br.at[i, 2], b_send, b_recv.at[i, 2], at_z(1)).start()
        rdma(s.at[i, rows_of(-1), gate], br.at[i, 3], b_send, b_recv.at[i, 3], at_z(-1)).start()

    def combine(i):
        for n, d, cols in ((0, 1, gate), (1, -1, up)):
            wait_recv(br.at[i, n], b_recv.at[i, n])
            cs[i, n] = (s[i, rows_of(d), cols].astype(F32) + br[i, n].astype(F32)).astype(BF)
            rdma(cs.at[i, n], br.at[i, 4 + n], cs_send, b_recv.at[i, 4 + n], at_z(d)).start()

    def finish(i):
        for n in (2, 3, 4, 5):
            wait_recv(br.at[i, n], b_recv.at[i, n])
        g = s[i, rows_of(0), gate].astype(F32) + br[i, 4].astype(F32) + br[i, 3].astype(F32)
        u = s[i, rows_of(0), up].astype(F32) + br[i, 5].astype(F32) + br[i, 2].astype(F32)
        hid[i, rows_of(0), mine] = (g / (1.0 + jnp.exp(-g)) * u).astype(BF)
        block = hid.at[i, rows_of(0), mine]
        rdma(block, block, c_send, c_recv.at[i, 0], at_z(1)).start()
        rdma(block, block, c_send, c_recv.at[i, 1], at_z(-1)).start()

    def half_rows(d, n):
        return pl.ds(pl.multiple_of(lax.rem(z + d + 4, 4) * ROWS + n * 16, 16), 16)

    def forward(i):
        for n, d in ((0, -1), (1, 1)):
            wait_recv(hid.at[i, rows_of(d), mine], c_recv.at[i, n])
            block = hid.at[i, half_rows(d, n), mine]
            rdma(block, block, c_send, c_recv.at[i, 2 + n], at_z(-d)).start()

    def pair(i):
        for n in (0, 1):
            wait_recv(hid.at[i, half_rows(2, n), mine], c_recv.at[i, 2 + n])
        block = hid.at[i, :, mine]
        rdma(block, block, hs_send, hs_recv.at[i], sibling).start()

    def second_matmul(i):
        other = pl.ds(pl.multiple_of((1 - c) * FH, 128), FH)
        wait_recv(hid.at[i, :, other], hs_recv.at[i])

        @pl.loop(0, KB // 256)
        def _(n):
            cols = pl.ds(pl.multiple_of(n * 256, 256), 256)
            t = jnp.dot(hid[i], wd[:, cols], preferred_element_type=F32)
            ds[i, :, cols] = t.astype(BF)

        @pl.when(i < LAST)
        def _():
            o = i + 1
            dev = at_xy(x + o % 4, y + o // 4)
            rdma(ds.at[i], dr.at[i], d_send, d_recv.at[i], dev).start()

    def gather_sum(i):
        wait_recv(dr.at[i], d_recv.at[i])
        acc[...] += dr[i].astype(F32)

    def at(i, low, high, body):
        @pl.when(jnp.logical_and(i >= low, i < high))
        def _():
            body(i - low)

    def step(t, carry):
        pl.when(t == 1)(events1)
        pl.when(t == 2)(events2)
        pl.when(t == 3)(events3)
        pl.when(t == 6)(events4)
        at(t, 0, STEPS, first_matmul)
        at(t, 1, STEPS + 1, combine)
        at(t, 2, STEPS + 2, finish)
        at(t, 3, STEPS + 3, forward)
        at(t, 4, STEPS + 4, pair)
        pl.when(t == 5)(own_wd.wait)
        at(t, 5, STEPS + 5, second_matmul)
        at(t, 7, LAST + 7, gather_sum)
        return carry

    lax.fori_loop(0, LAST + 7, step, 0)
    out_ref[...] = (acc[...] + ds[LAST].astype(F32)).astype(BF)

    for _ in rows:
        pass
    wait_send(sq.at[0:7], sq_send)
    for g in range(2):
        wait_send(w.at[c, :, g * FH:(g + 1) * FH], w_send.at[g])
    wait_send(a.at[0:15, c], a_send)
    wait_send(a.at[:, c], as_send)
    wait_send(s.at[:, :, gate], b_send)
    wait_send(cs, cs_send)
    wait_send(hid.at[:, 0:3 * ROWS, gate], c_send)
    wait_send(hid.at[:, :, gate], hs_send)
    wait_send(ds.at[0:LAST], d_send)


def local(hidden_state, norm_gain, gate_up_weight, down_weight):
    wt = jnp.transpose(gate_up_weight, (1, 0, 2))
    dma = pltpu.SemaphoreType.DMA
    any_, vmem = pl.BlockSpec(memory_space=pl.ANY), pl.BlockSpec(memory_space=pltpu.VMEM)
    return pl.pallas_call(
        kernel,
        out_shape=jax.ShapeDtypeStruct((TOK, KB), BF),
        in_specs=[vmem, vmem, any_, any_],
        out_specs=vmem,
        scratch_shapes=[
            pltpu.VMEM((STEPS, 2, TOK, KB), BF),
            pltpu.VMEM((2, KB, 2 * FH), BF),
            pltpu.VMEM((2 * FH, KB), BF),
            pltpu.VMEM((STEPS, TOK, 2 * FH), BF),
            pltpu.VMEM((STEPS, 6, ROWS, FH), BF),
            pltpu.VMEM((STEPS, 2, ROWS, FH), BF),
            pltpu.VMEM((STEPS, TOK, 2 * FH), BF),
            pltpu.VMEM((STEPS, TOK, KB), BF),
            pltpu.VMEM((LAST, TOK, KB), BF),
            pltpu.VMEM((TOK, KB), F32),
            pltpu.VMEM((8, 8, 128), F32),
            dma, dma((8,)), dma, dma((STEPS, 2)), dma, dma((STEPS,)),
            dma((2,)), dma((2,)), dma((2,)), dma,
            dma, dma((STEPS, 6)), dma, dma((STEPS, 4)), dma, dma, dma((STEPS,)), dma, dma((STEPS,)),
        ],
        compiler_params=pltpu.CompilerParams(
            collective_id=0, has_side_effects=True, vmem_limit_bytes=60 * 1024 * 1024
        ),
    )(hidden_state, norm_gain.reshape(1, KB), wt, down_weight)


def solution(mesh):
    return jax.shard_map(
        local,
        mesh=mesh,
        in_specs=(
            P(("col", "depth"), "row"),
            P("row"),
            P("row", None, ("col", "depth")),
            P(("col", "depth"), "row"),
        ),
        out_specs=P(("col", "depth"), "row"),
        check_vma=False,
    )
```

time: 396 us -> 173 us (0.44)
  the two profiles are of different devices: /device:TPU:0 before, /device:TPU:14 now
where the time goes in v1:
time: 173 us
  Pallas kernels  165 us (95%)
  local copies, waits for them, and re-layouts  8.64 us (5%)
    pallas_call x1, Pallas kernels, local(): pl.pallas_call(kernel, out_shape=jax.ShapeDtypeStruct((TOK, KB), BF), in_...  165 us
    unnamed x2, local copies, waits for them, and re-layouts  8.64 us

profile of v1, /device:TPU:14, one launch (start us, length us, event | category | flops | bytes accessed | tf_op | source)
XLA Modules:
  0.0 173.3 jit_solution(12806166694913861816)
XLA Ops:
  0.0 7.0 %copy.7 = bf16[1024,2,1792]{2,0,1:T(8,128)(2,1)} copy(bf16[1024,2,1792]{2,1,0:T(2,128)(2,1)} %param.6) | data formatting | bytes 14680064 | tf_op args[2]
  7.0 164.7 %shard_map.46 = bf16[128,1024]{1,0:T(8,128)(2,1)} custom-call(bf16[128,1024]{1,0:T(8,128)(2,1)} %h_ref.1, f32[1,1024]{1,0:T(1,128)} %bitcast.5, bf16[2,1024,1792]{2,1,0:T(8,128)(2,1)} %bitcast.4, bf16[1792,1024]{1,0:T(8,128)(2,1)} %wd_ref.1), custom_call_target="tpu_custom_call" | custom-call | tf_op jit(solution)/shard_map/pallas_call | solution.py:310
  171.6 1.7 copy.9

commit v2 on v0

v2 whole, which is shorter than its diff:
```python
import functools

import jax
import jax.numpy as jnp
from jax import lax
from jax.experimental import pallas as pl
from jax.experimental.pallas import tpu as pltpu
from jax.sharding import PartitionSpec as P

D = 8192
TOK = 128
KB = 1024
FH = 896
STEPS = 16
COMBINE, FINISH, FORWARD, PAIR, LAG = 2, 3, 4, 5, 6
ROWS = TOK // 4
OWN = 0
MESH = pl.DeviceIdType.MESH
BF, F32 = jnp.bfloat16, jnp.float32


def kernel(
    h_ref, gain_ref, wg_ref, wd_ref, out_ref,
    a, raw, w, wd, s, br, cs, hid, ds, df, dn, ys, xf, xn, acc, sq, sc,
    sq_send, sq_recv, sc_send, sc_recv, a_send, a_recv, as_send, as_recv,
    w_local, w_send, w_recv, wd_sem,
    b_send, b_recv, c_send, c_recv, cs_send, hs_send, hs_recv, d_send, y_recv, x_recv,
):
    col, depth, row = lax.axis_index("col"), lax.axis_index("depth"), lax.axis_index("row")
    x, y = col // 2, depth * 2 + col % 2
    z, c = row // 2, row % 2

    def at_xy(nx, ny):
        nx, ny = lax.rem(nx + 8, 4), lax.rem(ny + 8, 4)
        return {"col": nx * 2 + ny % 2, "depth": ny // 2}

    def at_z(d, other=0):
        core = c if not other else 1 - c
        return {"row": lax.rem(z + d + 4, 4) * 2 + core}

    sibling = at_z(0, 1)

    def rdma(src, dst, ssem, rsem, dev):
        return pltpu.make_async_remote_copy(
            src_ref=src, dst_ref=dst, send_sem=ssem, recv_sem=rsem, device_id=dev, device_id_type=MESH
        )

    def wait_recv(ref, sem, dev=sibling):
        rdma(ref, ref, a_send, sem, dev).wait_recv()

    def wait_send(ref, sem, dev=sibling):
        rdma(ref, ref, sem, sem, dev).wait_send()

    def wide(v):
        return v.astype(F32)

    barrier = pltpu.get_barrier_semaphore()
    plane = range(1, 16)
    peers = [at_xy(x + o // 4, y + o % 4) for o in plane]
    rows = [{"row": lax.rem(row + d, 8)} for d in range(1, 8)]

    def columns(core):
        return pl.ds(pl.multiple_of(core * FH, 128), FH)

    own_w = pltpu.make_async_copy(wg_ref.at[:, :, columns(c)], raw.at[c], w_local)
    own_w.start()
    own_wd = pltpu.make_async_copy(wd_ref, wd, wd_sem)
    own_wd.start()

    for dev in peers + rows:
        pl.semaphore_signal(barrier, inc=1, device_id=dev, device_id_type=MESH)

    lanes = jnp.zeros((TOK, 128), F32)
    for k in range(KB // 128):
        cols = slice(k * 128, (k + 1) * 128)
        v = h_ref[:, cols].astype(F32)
        a[OWN, c, :, cols] = (v * gain_ref[0:1, cols]).astype(BF)
        acc[:, cols] = v
        lanes = lanes + v * v
    sums = jnp.sum(lanes.T, axis=0, keepdims=True)
    sq[row] = jnp.broadcast_to(sums, (8, 128))

    pl.semaphore_wait(barrier, len(peers) + len(rows))

    half = TOK // 2

    def slot(dx, dy):
        return dx % 4 * 4 + dy % 4

    def place(dx, dy, n):
        dx = dx % 4
        return (slot(1 + 2 * n, dy), dx // 2) if dx % 2 else (slot(dx, dy), n)

    def part(at, n):
        return a.at[at, c, n * half:(n + 1) * half]

    def hop(dx, dy, n, ox, oy):
        dst = place(dx - ox, dy - oy, n)
        dev = at_xy(x + ox, y + oy)
        rdma(part(*place(dx, dy, n)), part(*dst), a_send, a_recv.at[dst[0], dst[1]], dev).start()

    def share(at):
        rdma(a.at[at, c], a.at[at, c], as_send, as_recv.at[at], sibling).start()

    def got(at, n):
        wait_recv(part(at, n), a_recv.at[at, n])

    def have(dx, dy):
        at = slot(dx, dy)
        got(at, 0)
        got(at, 1)
        share(at)

    def spread_y(*halves):
        for oy in (1, -1):
            for dx, n in halves:
                hop(dx, 0, n, 0, oy)

    def spread_x(dy, n):
        hop(0, dy, n, -1, 0)
        hop(0, dy, n, 1, 0)

    def first_x(k):
        if k == 0:
            spread_x(0, 0)
            spread_x(0, 1)
        elif k == 1:
            have(1, 0)
            spread_y((1, 0), (3, 0))
        elif k == 2:
            share(OWN)
            have(1, 1)
            hop(1, 1, 0, 0, -1)
            hop(3, 1, 0, 0, -1)
            have(3, 0)
            spread_y((1, 1), (3, 1))
            have(1, 3)
            hop(1, 0, 0, -1, 0)
            hop(3, 0, 1, 1, 0)
        elif k == 3:
            have(1, 2)
            have(3, 3)
            hop(1, 3, 1, 0, 1)
            hop(3, 3, 1, 0, 1)
            have(3, 1)
        elif k == 4:
            have(2, 0)
            spread_y((2, 0), (2, 1))
            have(3, 2)
        elif k == 5:
            have(2, 1)
            hop(2, 1, 0, 0, -1)
            have(2, 3)
            hop(2, 3, 1, 0, 1)
            spread_y((0, 0), (0, 1))
        elif k == 6:
            have(0, 1)
            hop(0, 1, 0, 0, -1)
            have(0, 3)
            hop(0, 3, 1, 0, 1)
        elif k == 7:
            have(2, 2)
        elif k == 8:
            have(0, 2)

    def first_y(k):
        if k == 0:
            spread_x(0, 0)
            spread_y((0, 0))
            spread_y((0, 1))
            spread_x(0, 1)
        elif k == 1:
            have(1, 0)
            got(slot(0, 1), 0)
            spread_x(1, 0)
            hop(0, 1, 0, 0, -1)
            got(slot(0, 3), 0)
            spread_x(3, 0)
        elif k == 2:
            share(OWN)
            got(slot(0, 2), 0)
            spread_x(2, 0)
            for dy in (1, 3):
                got(slot(0, dy), 1)
                share(slot(0, dy))
                spread_x(dy, 1)
            hop(0, 3, 1, 0, 1)
            have(1, 1)
            have(1, 3)
        elif k == 3:
            got(slot(0, 2), 1)
            share(slot(0, 2))
            spread_x(2, 1)
            have(1, 2)
            have(3, 0)
            for dy in (0, 1, 3, 2):
                hop(1, dy, 0, -1, 0)
        elif k == 4:
            for dy in (1, 3, 2):
                have(3, dy)
            for dy in (0, 1, 3, 2):
                hop(3, dy, 1, 1, 0)
        elif k == 7:
            for dy in (2, 1, 3, 0):
                have(2, dy)

    def gather(k):
        pl.when(c == 0)(functools.partial(first_x, k))
        pl.when(c == 1)(functools.partial(first_y, k))

    gather(0)
    for dev in rows:
        rdma(sq.at[row], sq.at[row], sq_send, sq_recv.at[row], dev).start()
    rdma(wg_ref.at[:, :, columns(1 - c)], raw.at[c], w_send, w_recv, sibling).start()

    def deal(core):
        @pl.loop(0, KB // 64)
        def _(n):
            ks = pl.ds(pl.multiple_of(n * 64, 64), 64)
            both = jnp.swapaxes(raw[core, ks], 0, 1)
            w[core, ks, 0:FH] = both[0]
            w[core, ks, FH:2 * FH] = both[1]

    own_w.wait()
    deal(c)
    def digit(n):
        return (1 + 3 * (n % 2)) * (1 + 15 * (n // 2))

    def offsets(i):
        g, j = i // 4, i % 4
        far_first = g // 2
        order = 180 - 126 * far_first
        dx = 45 // digit(g) % 4
        dy = order // digit(j) % 4
        return dx, dy

    def rows_of(d):
        return pl.ds(pl.multiple_of(lax.rem(z + d + 4, 4) * ROWS, ROWS), ROWS)

    def scales():
        for d in range(1, 8):
            r = lax.rem(row + d, 8)
            wait_recv(sq.at[r], sq_recv.at[r])
        total = sq[0]
        for r in range(1, 8):
            total = total + sq[r]
        scale = jnp.broadcast_to(lax.rsqrt(total[0:1] / D + 1e-05), (128, 128)).T
        for q in range(4):
            sc[OWN, q] = scale[q * ROWS:(q + 1) * ROWS]

        def give(dx, dy, q, n):
            dst = lax.rem(dx + 4, 4) * 4 + dy
            dev = at_xy(x - dx, y - dy)
            rdma(sc.at[OWN, q], sc.at[dst, q], sc_send, sc_recv.at[dst, n], dev).start()

        for dy in range(4):
            for n in range(2):
                give(1 + 2 * (z // 2), dy, 2 * n + z % 2, n)
        for dx, dy in ((2, 0), (2, 1), (2, 2), (2, 3), (0, 1), (0, 2), (0, 3)):
            give(dx, dy, z, 0)

    gather(1)
    wait_recv(raw.at[1 - c], w_recv)
    deal(1 - c)

    gate, up = slice(0, FH), slice(FH, 2 * FH)
    mine = columns(c)

    def first_matmul(i):
        dx, dy = offsets(i)
        at = dx * 4 + dy
        wait_recv(a.at[at, 1 - c], as_recv.at[at])

        @pl.loop(0, 2 * FH // 256)
        def _(n):
            cols = pl.ds(pl.multiple_of(n * 256, 256), 256)
            p = jnp.dot(a[at, 0], w[0, :, cols], preferred_element_type=F32)
            p += jnp.dot(a[at, 1], w[1, :, cols], preferred_element_type=F32)
            s[i, :, cols] = p.astype(BF)

        rdma(s.at[i, rows_of(2), gate], br.at[i, 0], b_send, b_recv.at[i, 0], at_z(1)).start()
        rdma(s.at[i, rows_of(2), up], br.at[i, 1], b_send, b_recv.at[i, 1], at_z(-1)).start()
        rdma(s.at[i, rows_of(1), up], br.at[i, 2], b_send, b_recv.at[i, 2], at_z(1)).start()
        rdma(s.at[i, rows_of(-1), gate], br.at[i, 3], b_send, b_recv.at[i, 3], at_z(-1)).start()

    def combine(i):
        for n, d, cols in ((0, 1, gate), (1, -1, up)):
            wait_recv(br.at[i, n], b_recv.at[i, n])
            cs[i, n] = (s[i, rows_of(d), cols].astype(F32) + br[i, n].astype(F32)).astype(BF)
            rdma(cs.at[i, n], br.at[i, 4 + n], cs_send, b_recv.at[i, 4 + n], at_z(d)).start()

    def finish(i):
        for n in (2, 3, 4, 5):
            wait_recv(br.at[i, n], b_recv.at[i, n])
        dx, dy = offsets(i)
        mixed, n = 1 - i // 8, i // 4
        at = (mixed * (1 + 2 * (z // 2)) + (1 - mixed) * dx) * 4 + dy
        q = mixed * (2 * n + z % 2) + (1 - mixed) * z

        @pl.when(at != OWN)
        def _():
            wait_recv(sc.at[at, q], sc_recv.at[at, mixed * n])

        scale = sc[at, q]
        for k in range(FH // 128):
            cols = slice(k * 128, (k + 1) * 128)
            ups = slice(FH + k * 128, FH + (k + 1) * 128)
            g = (wide(s[i, rows_of(0), cols]) + wide(br[i, 4, :, cols]) + wide(br[i, 3, :, cols])) * scale
            u = (wide(s[i, rows_of(0), ups]) + wide(br[i, 5, :, cols]) + wide(br[i, 2, :, cols])) * scale
            to = pl.ds(pl.multiple_of(c * FH + k * 128, 128), 128)
            hid[i, rows_of(0), to] = (g / (1.0 + jnp.exp(-g)) * u).astype(BF)
        block = hid.at[i, rows_of(0), mine]
        rdma(block, block, c_send, c_recv.at[i, 0], at_z(1)).start()
        rdma(block, block, c_send, c_recv.at[i, 1], at_z(-1)).start()

    def half_rows(d, n):
        return pl.ds(pl.multiple_of(lax.rem(z + d + 4, 4) * ROWS + n * 16, 16), 16)

    def forward(i):
        for n, d in ((0, -1), (1, 1)):
            wait_recv(hid.at[i, rows_of(d), mine], c_recv.at[i, n])
            block = hid.at[i, half_rows(d, n), mine]
            rdma(block, block, c_send, c_recv.at[i, 2 + n], at_z(-d)).start()

    def pair(i):
        for n in (0, 1):
            wait_recv(hid.at[i, half_rows(2, n), mine], c_recv.at[i, 2 + n])
        block = hid.at[i, :, mine]
        rdma(block, block, hs_send, hs_recv.at[i], sibling).start()

    def second_matmul(i):
        wait_recv(hid.at[i, :, columns(1 - c)], hs_recv.at[i])

        @pl.loop(0, KB // 256)
        def _(n):
            cols = pl.ds(pl.multiple_of(n * 256, 256), 256)
            t = jnp.dot(hid[i], wd[:, cols], preferred_element_type=F32)
            ds[i, :, cols] = t.astype(BF)

    def ring(d):
        return at_xy(x, y + d)

    def line(d):
        return at_xy(x + d, y)

    top, low = slice(0, half), slice(half, TOK)

    def y_far(g, i):
        rdma(ds.at[i, top], df.at[g, 0], d_send, y_recv.at[g, 0], ring(1)).start()
        rdma(ds.at[i, low], df.at[g, 1], d_send, y_recv.at[g, 1], ring(-1)).start()

    def y_near(g, i, n):
        rows = (top, low)[n]
        wait_recv(df.at[g, n], y_recv.at[g, n])
        ds[i, rows] = (wide(ds[i, rows]) + wide(df[g, n])).astype(BF)
        rdma(ds.at[i], dn.at[g, n], d_send, y_recv.at[g, 2 + n], ring(1 - 2 * n)).start()

    def y_sum(g, i):
        for n in range(2):
            wait_recv(dn.at[g, n], y_recv.at[g, 2 + n])
        ys[g] = (wide(ds[i]) + wide(dn[g, 0]) + wide(dn[g, 1])).astype(BF)

    def x_far():
        rdma(ys.at[2, top], xf.at[0], d_send, x_recv.at[0], line(1)).start()
        rdma(ys.at[2, low], xf.at[1], d_send, x_recv.at[1], line(-1)).start()

    def x_near(n):
        rows = (top, low)[n]
        wait_recv(xf.at[n], x_recv.at[n])
        ys[n, rows] = (wide(ys[n, rows]) + wide(xf[n])).astype(BF)
        for m in range(2):
            to = xn.at[n, (top, low)[m]]
            rdma(ys.at[m, rows], to, d_send, x_recv.at[2 + 2 * n + m], line(1 - 2 * n)).start()

    def branch_sums(t):
        def when(n, *bodies):
            @pl.when(t == LAG + n)
            def _():
                for body in bodies:
                    body()

        call = functools.partial
        for g in (0, 1):
            i = 4 * g
            when(i + 3, call(y_far, g, i + 3))
            when(i + 4, call(y_near, g, i + 1, 0), call(y_near, g, i + 2, 1))
            when(i + 6, call(y_sum, g, i))
        for g in (2, 3):
            i = 4 * g
            when(i, call(y_far, g, i))
            when(i + 1, call(y_near, g, i + 1, 0))
            when(i + 2, call(y_near, g, i + 2, 1))
        when(11, call(y_sum, 2, 11), x_far)
        when(13, call(x_near, 0), call(x_near, 1))

    def at(i, low, high, body):
        @pl.when(jnp.logical_and(i >= low, i < high))
        def _():
            body(i - low)

    def step(t, carry):
        pl.when(t == 1)(scales)
        at(t, COMBINE, STEPS + COMBINE, combine)
        at(t, FINISH, STEPS + FINISH, finish)
        at(t, FORWARD, STEPS + FORWARD, forward)
        at(t, PAIR, STEPS + PAIR, pair)
        for k in range(2, 9):
            pl.when(t == k - 1)(functools.partial(gather, k))
        at(t, 0, STEPS, first_matmul)
        pl.when(t == LAG)(own_wd.wait)
        at(t, LAG, STEPS + LAG, second_matmul)
        branch_sums(t)
        return carry

    lax.fori_loop(0, STEPS + LAG, step, 0)
    total = acc[...] + wide(ds[STEPS - 1])
    for n in range(2):
        for m in range(2):
            wait_recv(xn.at[n, (top, low)[m]], x_recv.at[2 + 2 * n + m])
        total += wide(xn[n])
    for n in range(2):
        wait_recv(dn.at[3, n], y_recv.at[3, 2 + n])
        total += wide(dn[3, n])
    out_ref[...] = total.astype(BF)

    wait_send(sq.at[0:7], sq_send)
    wait_send(raw.at[c], w_send)
    wait_send(sc.at[1:16, 0], sc_send)
    wait_send(a.at[0:15, c], a_send)
    wait_send(a.at[:, c], as_send)
    wait_send(s.at[:, :, gate], b_send)
    wait_send(cs, cs_send)
    wait_send(hid.at[:, 0:3 * ROWS, gate], c_send)
    wait_send(hid.at[:, :, gate], hs_send)
    wait_send(ds.at[0:15], d_send)


def local(hidden_state, norm_gain, gate_up_weight, down_weight):
    dma = pltpu.SemaphoreType.DMA
    any_, vmem = pl.BlockSpec(memory_space=pl.ANY), pl.BlockSpec(memory_space=pltpu.VMEM)
    return pl.pallas_call(
        kernel,
        out_shape=jax.ShapeDtypeStruct((TOK, KB), BF),
        in_specs=[vmem, vmem, any_, any_],
        out_specs=vmem,
        scratch_shapes=[
            pltpu.VMEM((STEPS, 2, TOK, KB), BF),
            pltpu.VMEM((2, KB, 2, FH), BF),
            pltpu.VMEM((2, KB, 2 * FH), BF),
            pltpu.VMEM((2 * FH, KB), BF),
            pltpu.VMEM((STEPS, TOK, 2 * FH), BF),
            pltpu.VMEM((STEPS, 6, ROWS, FH), BF),
            pltpu.VMEM((STEPS, 2, ROWS, FH), BF),
            pltpu.VMEM((STEPS, TOK, 2 * FH), BF),
            pltpu.VMEM((STEPS, TOK, KB), BF),
            pltpu.VMEM((4, 2, TOK // 2, KB), BF),
            pltpu.VMEM((4, 2, TOK, KB), BF),
            pltpu.VMEM((3, TOK, KB), BF),
            pltpu.VMEM((2, TOK // 2, KB), BF),
            pltpu.VMEM((2, TOK, KB), BF),
            pltpu.VMEM((TOK, KB), F32),
            pltpu.VMEM((8, 8, 128), F32),
            pltpu.VMEM((STEPS, 4, ROWS, 128), F32),
            dma, dma((8,)), dma, dma((STEPS, 2)), dma, dma((STEPS, 2)), dma, dma((STEPS,)),
            dma, dma, dma, dma,
            dma, dma((STEPS, 6)), dma, dma((STEPS, 4)), dma, dma, dma((STEPS,)), dma, dma((4, 4)), dma((6,)),
        ],
        compiler_params=pltpu.CompilerParams(
            collective_id=0, has_side_effects=True, vmem_limit_bytes=60 * 1024 * 1024
        ),
    )(hidden_state, norm_gain.reshape(1, KB), gate_up_weight, down_weight)


def solution(mesh):
    return jax.shard_map(
        local,
        mesh=mesh,
        in_specs=(
            P(("col", "depth"), "row"),
            P("row"),
            P("row", None, ("col", "depth")),
            P(("col", "depth"), "row"),
        ),
        out_specs=P(("col", "depth"), "row"),
        check_vma=False,
    )
```

time: 396 us -> 137 us (0.35)
  waiting for transfers between devices: 324 us -> 0 us
  Pallas kernels: 0 us -> 135 us
  matrix products: 34.6 us -> 0 us
  blocking collectives: 16 us -> 0 us
  between operations: 13.1 us -> 0.01 us
  other arithmetic: 7.84 us -> 0 us
    reduce_scatter x2 -> x0, waiting for transfers between devices: 182 us -> none  [the longest x1 100 us: local(): lax.psum_scatter(terms.astype(jnp.bfloat16), ('col', 'depth'), scatter_di...]
    all_gather x2 -> x0, waiting for transfers between devices: 143 us -> none  [the longest x1 97.5 us: local(): lax.all_gather(normed, ('col', 'depth'), axis=0, tiled=True)]
    pallas_call x0 -> x1, Pallas kernels: none -> 135 us  [local(): pl.pallas_call(kernel, out_shape=jax.ShapeDtypeStruct((TOK, KB), BF), in_...]
    dot_general x2 -> x0, matrix products: 34.6 us -> none  [the longest x1 22.3 us: local(): jnp.einsum('td,dkf->tkf', lax.all_gather(normed, ('col', 'depth'), axis=0...]
    psum x1 -> x0, blocking collectives: 16 us -> none  [local(): squares = lax.psum(jnp.sum(wide * wide, axis=1), 'row')]
    convert_element_type x4 -> x0, other arithmetic: 6.75 us -> none  [the longest x1 1.79 us: local(): normed = (wide * scale[:, None] * norm_gain[None, :]).astype(jnp.bfloat16)]
  transfers between devices with their start and end apart: 4 -> 0, of which waited for: 4 -> 0; matrix products, arithmetic and copies ran while one was open for 0% -> 0% of each run, Pallas kernels for 0% -> 0%
where the time goes in v2:
time: 137 us
  Pallas kernels  135 us (99%)
  local copies, waits for them, and re-layouts  1.67 us (1%)
    pallas_call x1, Pallas kernels, local(): pl.pallas_call(kernel, out_shape=jax.ShapeDtypeStruct((TOK, KB), BF), in_...  135 us

profile of v2, /device:TPU:0, one launch (start us, length us, event | category | flops | bytes accessed | tf_op | source)
XLA Modules:
  0.0 137.0 jit_solution(5862230997990305302)
XLA Ops:
  0.0 135.3 %shard_map.46 = bf16[128,1024]{1,0:T(8,128)(2,1)} custom-call(bf16[128,1024]{1,0:T(8,128)(2,1)} %h_ref.1, f32[1,1024]{1,0:T(1,128)} %bitcast.1, bf16[1024,2,1792]{2,1,0:T(2,128)(2,1)} %wg_ref.1, bf16[1792,1024]{1,0:T(8,128)(2,1)} %wd_ref.1), custom_call_target="tpu_custom_call" | custom-call | tf_op jit(solution)/shard_map/pallas_call | solution.py:441
  135.3 1.7 %copy.6 = bf16[128,1024]{1,0:T(8,128)(2,1)} copy(bf16[128,1024]{1,0:T(8,128)(2,1)} %shard_map.46) | data formatting | bytes 524288

commit v3 on v2

--- a/solution.py
+++ b/solution.py
@@ -271,17 +271,18 @@
         at = dx * 4 + dy
         wait_recv(a.at[at, 1 - c], as_recv.at[at])
 
-        @pl.loop(0, 2 * FH // 256)
-        def _(n):
+        def tile(n):
             cols = pl.ds(pl.multiple_of(n * 256, 256), 256)
             p = jnp.dot(a[at, 0], w[0, :, cols], preferred_element_type=F32)
             p += jnp.dot(a[at, 1], w[1, :, cols], preferred_element_type=F32)
             s[i, :, cols] = p.astype(BF)
 
+        pl.loop(0, 4)(tile)
         rdma(s.at[i, rows_of(2), gate], br.at[i, 0], b_send, b_recv.at[i, 0], at_z(1)).start()
+        rdma(s.at[i, rows_of(-1), gate], br.at[i, 3], b_send, b_recv.at[i, 3], at_z(-1)).start()
+        pl.loop(4, 7)(tile)
         rdma(s.at[i, rows_of(2), up], br.at[i, 1], b_send, b_recv.at[i, 1], at_z(-1)).start()
         rdma(s.at[i, rows_of(1), up], br.at[i, 2], b_send, b_recv.at[i, 2], at_z(1)).start()
-        rdma(s.at[i, rows_of(-1), gate], br.at[i, 3], b_send, b_recv.at[i, 3], at_z(-1)).start()
 
     def combine(i):
         for n, d, cols in ((0, 1, gate), (1, -1, up)):
@@ -350,14 +351,23 @@
         rdma(ds.at[i, low], df.at[g, 1], d_send, y_recv.at[g, 1], ring(-1)).start()
 
     def y_near(g, i, n):
-        rows = (top, low)[n]
+        halves = (top, low)
+        dev = ring(1 - 2 * n)
+        rest = halves[1 - n]
+        rdma(ds.at[i, rest], dn.at[g, n, rest], d_send, y_recv.at[g, 4 + n], dev).start()
+        rows = halves[n]
         wait_recv(df.at[g, n], y_recv.at[g, n])
         ds[i, rows] = (wide(ds[i, rows]) + wide(df[g, n])).astype(BF)
-        rdma(ds.at[i], dn.at[g, n], d_send, y_recv.at[g, 2 + n], ring(1 - 2 * n)).start()
+        rdma(ds.at[i, rows], dn.at[g, n, rows], d_send, y_recv.at[g, 2 + n], dev).start()
+
+    def y_got(g):
+        for n in range(2):
+            halves = (top, low)
+            wait_recv(dn.at[g, n, halves[1 - n]], y_recv.at[g, 4 + n])
+            wait_recv(dn.at[g, n, halves[n]], y_recv.at[g, 2 + n])
 
     def y_sum(g, i):
-        for n in range(2):
-            wait_recv(dn.at[g, n], y_recv.at[g, 2 + n])
+        y_got(g)
         ys[g] = (wide(ds[i]) + wide(dn[g, 0]) + wide(dn[g, 1])).astype(BF)
 
     def x_far():
@@ -418,8 +428,8 @@
         for m in range(2):
             wait_recv(xn.at[n, (top, low)[m]], x_recv.at[2 + 2 * n + m])
         total += wide(xn[n])
+    y_got(3)
     for n in range(2):
-        wait_recv(dn.at[3, n], y_recv.at[3, 2 + n])
         total += wide(dn[3, n])
     out_ref[...] = total.astype(BF)
 
@@ -463,7 +473,7 @@
             pltpu.VMEM((STEPS, 4, ROWS, 128), F32),
             dma, dma((8,)), dma, dma((STEPS, 2)), dma, dma((STEPS, 2)), dma, dma((STEPS,)),
             dma, dma, dma, dma,
-            dma, dma((STEPS, 6)), dma, dma((STEPS, 4)), dma, dma, dma((STEPS,)), dma, dma((4, 4)), dma((6,)),
+            dma, dma((STEPS, 6)), dma, dma((STEPS, 4)), dma, dma, dma((STEPS,)), dma, dma((4, 6)), dma((6,)),
         ],
         compiler_params=pltpu.CompilerParams(
             collective_id=0, has_side_effects=True, vmem_limit_bytes=60 * 1024 * 1024

time: 137 us -> 135 us (0.985)
  Pallas kernels: 135 us -> 133 us
    pallas_call x1, Pallas kernels: 135 us -> 133 us  [local(): pl.pallas_call(kernel, out_shape=jax.ShapeDtypeStruct((TOK, KB), BF), in_...]
where the time goes in v3:
time: 135 us
  Pallas kernels  133 us (99%)
  local copies, waits for them, and re-layouts  1.67 us (1%)
    pallas_call x1, Pallas kernels, local(): pl.pallas_call(kernel, out_shape=jax.ShapeDtypeStruct((TOK, KB), BF), in_...  133 us

profile of v3, /device:TPU:0, one launch (start us, length us, event | category | flops | bytes accessed | tf_op | source)
XLA Modules:
  0.0 135.0 jit_solution(714091216460598217)
XLA Ops:
  0.0 133.3 %shard_map.46 = bf16[128,1024]{1,0:T(8,128)(2,1)} custom-call(bf16[128,1024]{1,0:T(8,128)(2,1)} %h_ref.1, f32[1,1024]{1,0:T(1,128)} %bitcast.1, bf16[1024,2,1792]{2,1,0:T(2,128)(2,1)} %wg_ref.1, bf16[1792,1024]{1,0:T(8,128)(2,1)} %wd_ref.1), custom_call_target="tpu_custom_call" | custom-call | tf_op jit(solution)/shard_map/pallas_call | solution.py:451
  133.3 1.7 %copy.6 = bf16[128,1024]{1,0:T(8,128)(2,1)} copy(bf16[128,1024]{1,0:T(8,128)(2,1)} %shard_map.46) | data formatting | bytes 524288
